TPU v7x, 128 devices: a whole 4x4x4 slice. The times are simulated.
128 devices in a mesh: group: 8 (over y_hi, x), row: 16 (over z, y_lo, core).
Axes of the slice: x: 4, y: 4 (y_hi: 2, y_lo: 2; y = y_hi * 2 + y_lo), z: 4, core: 2. Of those that a mesh axis runs over, the one named last changes fastest.
Arguments:
- embeds: bfloat16 [65536, 768], P(('group', 'row')), may hold values from -120 to 120
- member: int32 [65536], P(('group', 'row')), may hold values from 0 to 7, as said below
Outputs:
- nearest: float32 [65536], P(('group', 'row'))
Inputs may be any that keep to these rules, and one draw needn't show every extreme that they name: `member`: rows come in aligned blocks of 512; no cluster takes more than 128 rows of one block. For each remainder of the block index modulo the row axis's size, one cluster takes exactly 128 rows of every block with that remainder.
All inputs are finite; a program needn't handle non-finite values.
Results may differ from a plain program's by a relative error of at most 0.00056.
Values may be sent and summed in bfloat16 or wider, within the bound.
No kernel may reach another device: no remote copies, remote signals or barrier semaphores. Data moves between devices by JAX's collectives and lax.ppermute only.
A program may use at most 128 MiB of HBM per device.

v0:
```python
import math
import jax
import jax.numpy as jnp
from jax import lax
from jax.sharding import PartitionSpec as P

absent = -4.0


def block_maxima(own_rows, own_flags, column_rows, column_flags, own_ids, column_ids):
    stride = math.gcd(column_rows.shape[0], 2048)
    number = column_rows.shape[0] // stride
    pieces = column_rows.reshape(number, stride, column_rows.shape[1])
    piece_flags = column_flags.reshape(number, stride)
    piece_ids = column_ids.reshape(number, stride)
    own_keep = own_flags > 0

    def visit(row_best, item):
        piece_rows, flags_part, ids_part = item
        scores = lax.dot_general(
            own_rows, piece_rows, (((1,), (1,)), ((), ())), preferred_element_type=jnp.float32
        )
        keep = (
            own_keep[:, None] & (flags_part[None, :] > 0) & (own_ids[:, None] != ids_part[None, :])
        )
        masked = jnp.where(keep, scores, absent)
        return (jnp.maximum(row_best, jnp.max(masked, axis=1)), jnp.max(masked, axis=0))

    start_best = jnp.full((own_rows.shape[0],), absent, jnp.float32)
    row_best, column_best = lax.scan(visit, start_best, (pieces, piece_flags, piece_ids))
    return (row_best, column_best.reshape(-1))


def on_device(embeds, member):
    groups = lax.axis_size("group")
    block_rows = embeds.shape[0]
    per_cluster = 2 * block_rows // groups
    capacity = groups * per_cluster
    values = embeds.astype(jnp.float32)
    normed = (values * lax.rsqrt(jnp.sum(values * values, axis=1, keepdims=True) + 1e-06)).astype(
        jnp.bfloat16
    )
    hits = (member[:, None] == jnp.arange(groups, dtype=jnp.int32)[None, :]).astype(jnp.int32)
    ranking = jnp.sum(jnp.cumsum(hits, axis=0) * hits, axis=1) - 1
    target = member * per_cluster + ranking
    placer = (jnp.arange(capacity, dtype=jnp.int32)[:, None] == target[None, :]).astype(
        jnp.bfloat16
    )
    outgoing = jnp.dot(placer, normed, preferred_element_type=jnp.float32).astype(jnp.bfloat16)
    counts = jnp.sum(hits, axis=0)
    filled = (jnp.arange(per_cluster, dtype=jnp.int32)[None, :] < counts[:, None]).astype(
        jnp.bfloat16
    )
    arrived, arrived_flags = (
        lax.all_to_all(
            outgoing.reshape(groups, per_cluster, -1),
            "group",
            split_axis=0,
            concat_axis=0,
            tiled=True,
        ),
        lax.all_to_all(filled, "group", split_axis=0, concat_axis=0, tiled=True),
    )
    own_rows = arrived.reshape(capacity, -1)
    own_flags = arrived_flags.reshape(capacity)
    own_ids = lax.axis_index("row") * capacity + jnp.arange(capacity, dtype=jnp.int32)
    initial = jnp.full((capacity,), absent, jnp.float32)
    column_rows = lax.all_gather(own_rows, "row", axis=0, tiled=True)
    column_flags = lax.all_gather(own_flags, "row", axis=0, tiled=True)
    column_ids = jnp.arange(column_rows.shape[0], dtype=jnp.int32)
    found, unused_columns = block_maxima(
        own_rows, own_flags, column_rows, column_flags, own_ids, column_ids
    )
    nearest = jnp.maximum(initial, found)
    homeward = lax.all_to_all(
        nearest.reshape(groups, per_cluster), "group", split_axis=0, concat_axis=0, tiled=True
    )
    return homeward.reshape(-1)[target]


def solution(mesh):
    in_specs = (P(("group", "row"), None), P(("group", "row")))
    out_specs = P(("group", "row"))
    return jax.shard_map(
        on_device, mesh=mesh, in_specs=in_specs, out_specs=out_specs, check_vma=False
    )
```

profile of v0, /device:TPU:0, one launch (start us, length us, event | category | flops | bytes accessed | tf_op | source)
XLA Modules:
  0.0 246.7 jit_solution(17565139092833224877)
XLA Ops:
  6.5 0.7 fusion.14
  7.2 1.1 reduce-window.6
  8.6 0.9 fusion.13
  9.5 0.7 compare_select_fusion
  10.2 1.4 fusion.8
  11.5 2.3 fusion.7
  13.8 29.7 %all_to_all.20 = bf16[8,128,768]{2,1,0:T(8,128)(2,1)} all-to-all(bf16[8,128,768]{2,1,0:T(8,128)(2,1)S(1)} %bitcast.34), channel_id=1, replica_groups=mesh['group'=8,'row'=16] {'group'}, dimensions={0} | all-to-all | bytes 3145728 | tf_op jit(solution)/shard_map/all_to_all | solution.py:55
  43.6 0.7 compare_convert_fusion
  44.3 3.3 %all-to-all-start = ((bf16[8,1,128]{2,1,0:T(2,128)(2,1)}), bf16[8,1,128]{2,1,0:T(2,128)(2,1)S(1)}, u32[]{:S(2)}, u32[]{:S(2)}) async-start(bf16[8,1,128]{2,1,0:T(2,128)(2,1)} %compare_convert_fusion), calls=%async_computation | async-start | bytes 8192 | tf_op jit(solution)/shard_map/all_to_all | solution.py:62
  47.6 7.6 %all-to-all-done = bf16[8,1,128]{2,1,0:T(2,128)(2,1)S(1)} async-done(((bf16[8,1,128]{2,1,0:T(2,128)(2,1)}), bf16[8,1,128]{2,1,0:T(2,128)(2,1)S(1)}, u32[]{:S(2)}, u32[]{:S(2)}) %all-to-all-start) | async-done | bytes 2080 | tf_op jit(solution)/shard_map/all_to_all | solution.py:62
  55.2 20.3 %all_gather.6 = bf16[16384]{0:T(1024)(128)(2,1)S(1)} all-gather(bf16[1024]{0:T(1024)(128)(2,1)S(1)} %bitcast.37), channel_id=1, replica_groups=mesh['group'=8,'row'=16] {'row'}, dimensions={0}, use_global_device_ids=true | all-gather | bytes 34816 | tf_op jit(solution)/shard_map/all_gather | solution.py:69
  75.5 97.8 %all-gather.2.cloned.1.call-done = bf16[16384,768]{1,0:T(8,128)(2,1)} async-done(((bf16[1024,768]{1,0:T(8,128)(2,1)}), bf16[16384,768]{1,0:T(8,128)(2,1)}) %all-gather.2.cloned.1.call-update) | async-done | bytes 25165840 | tf_op jit(solution)/shard_map/all_gather | solution.py:68
  173.3 48.2 %while.11 = (s32[]{:T(128)}, f32[1024]{0:T(1024)S(1)}, pred[1024]{0:T(1024)(128)(4,1)S(1)}, bf16[8,2048]{1,0:T(8,128)(2,1)S(1)}, s32[8,2048]{1,0:T(8,128)S(1)}, ...) while((s32[]{:T(128)}, f32[1024]{0:T(1024)S(1)}, ...), condition=%wide.region_7.8_spmd.clone, body=%wide.region_5.7_spmd.clone.sunk | while | flops 3231719424 | bytes 4777595 | solution.py:30
  173.4 5.9 %fusion.21 = f32[1024]{0:T(1024)S(1)} fusion(bf16[1024,768]{1,0:T(8,128)(2,1)} %get-tuple-element.173, s32[1024]{0:T(1024)S(1)} %iota_add_fusion.2, s32[2048]{0:T(1024)S(1)} %bitcast.35, pred[1024]{0:T(1024)(128)(4,1)S(1)} %get-tuple-element.169, pred[2048]{0:T(1024)(128)(4,1)S(1)} %compare_reduce_fusion.2, ...), kind=kOutput, calls=%fused_computation.3.clone.1 | convolution fusion | flops 3231710208 | bytes 4738560 | tf_op jit(solution)/shard_map/while/body/eval_jaxpr/dot_general | solution.py:20
  179.4 5.9 %fusion.21 = f32[1024]{0:T(1024)S(1)} fusion(bf16[1024,768]{1,0:T(8,128)(2,1)} %get-tuple-element.173, s32[1024]{0:T(1024)S(1)} %iota_add_fusion.2, s32[2048]{0:T(1024)S(1)} %bitcast.35, pred[1024]{0:T(1024)(128)(4,1)S(1)} %get-tuple-element.169, pred[2048]{0:T(1024)(128)(4,1)S(1)} %compare_reduce_fusion.2, ...), kind=kOutput, calls=%fused_computation.3.clone.1 | convolution fusion | flops 3231710208 | bytes 4738560 | tf_op jit(solution)/shard_map/while/body/eval_jaxpr/dot_general | solution.py:20
  185.4 5.9 %fusion.21 = f32[1024]{0:T(1024)S(1)} fusion(bf16[1024,768]{1,0:T(8,128)(2,1)} %get-tuple-element.173, s32[1024]{0:T(1024)S(1)} %iota_add_fusion.2, s32[2048]{0:T(1024)S(1)} %bitcast.35, pred[1024]{0:T(1024)(128)(4,1)S(1)} %get-tuple-element.169, pred[2048]{0:T(1024)(128)(4,1)S(1)} %compare_reduce_fusion.2, ...), kind=kOutput, calls=%fused_computation.3.clone.1 | convolution fusion | flops 3231710208 | bytes 4738560 | tf_op jit(solution)/shard_map/while/body/eval_jaxpr/dot_general | solution.py:20
  191.5 5.9 %fusion.21 = f32[1024]{0:T(1024)S(1)} fusion(bf16[1024,768]{1,0:T(8,128)(2,1)} %get-tuple-element.173, s32[1024]{0:T(1024)S(1)} %iota_add_fusion.2, s32[2048]{0:T(1024)S(1)} %bitcast.35, pred[1024]{0:T(1024)(128)(4,1)S(1)} %get-tuple-element.169, pred[2048]{0:T(1024)(128)(4,1)S(1)} %compare_reduce_fusion.2, ...), kind=kOutput, calls=%fused_computation.3.clone.1 | convolution fusion | flops 3231710208 | bytes 4738560 | tf_op jit(solution)/shard_map/while/body/eval_jaxpr/dot_general | solution.py:20
  197.5 5.9 %fusion.21 = f32[1024]{0:T(1024)S(1)} fusion(bf16[1024,768]{1,0:T(8,128)(2,1)} %get-tuple-element.173, s32[1024]{0:T(1024)S(1)} %iota_add_fusion.2, s32[2048]{0:T(1024)S(1)} %bitcast.35, pred[1024]{0:T(1024)(128)(4,1)S(1)} %get-tuple-element.169, pred[2048]{0:T(1024)(128)(4,1)S(1)} %compare_reduce_fusion.2, ...), kind=kOutput, calls=%fused_computation.3.clone.1 | convolution fusion | flops 3231710208 | bytes 4738560 | tf_op jit(solution)/shard_map/while/body/eval_jaxpr/dot_general | solution.py:20
  203.5 5.9 %fusion.21 = f32[1024]{0:T(1024)S(1)} fusion(bf16[1024,768]{1,0:T(8,128)(2,1)} %get-tuple-element.173, s32[1024]{0:T(1024)S(1)} %iota_add_fusion.2, s32[2048]{0:T(1024)S(1)} %bitcast.35, pred[1024]{0:T(1024)(128)(4,1)S(1)} %get-tuple-element.169, pred[2048]{0:T(1024)(128)(4,1)S(1)} %compare_reduce_fusion.2, ...), kind=kOutput, calls=%fused_computation.3.clone.1 | convolution fusion | flops 3231710208 | bytes 4738560 | tf_op jit(solution)/shard_map/while/body/eval_jaxpr/dot_general | solution.py:20
  209.6 5.9 %fusion.21 = f32[1024]{0:T(1024)S(1)} fusion(bf16[1024,768]{1,0:T(8,128)(2,1)} %get-tuple-element.173, s32[1024]{0:T(1024)S(1)} %iota_add_fusion.2, s32[2048]{0:T(1024)S(1)} %bitcast.35, pred[1024]{0:T(1024)(128)(4,1)S(1)} %get-tuple-element.169, pred[2048]{0:T(1024)(128)(4,1)S(1)} %compare_reduce_fusion.2, ...), kind=kOutput, calls=%fused_computation.3.clone.1 | convolution fusion | flops 3231710208 | bytes 4738560 | tf_op jit(solution)/shard_map/while/body/eval_jaxpr/dot_general | solution.py:20
  215.6 5.9 %fusion.21 = f32[1024]{0:T(1024)S(1)} fusion(bf16[1024,768]{1,0:T(8,128)(2,1)} %get-tuple-element.173, s32[1024]{0:T(1024)S(1)} %iota_add_fusion.2, s32[2048]{0:T(1024)S(1)} %bitcast.35, pred[1024]{0:T(1024)(128)(4,1)S(1)} %get-tuple-element.169, pred[2048]{0:T(1024)(128)(4,1)S(1)} %compare_reduce_fusion.2, ...), kind=kOutput, calls=%fused_computation.3.clone.1 | convolution fusion | flops 3231710208 | bytes 4738560 | tf_op jit(solution)/shard_map/while/body/eval_jaxpr/dot_general | solution.py:20
  222.1 6.7 %all-to-all-start.2 = ((f32[8,1,128]{2,1,0:T(1,128)}), f32[8,1,128]{2,1,0:T(1,128)S(1)}, u32[]{:S(2)}, u32[]{:S(2)}) async-start(f32[8,1,128]{2,1,0:T(1,128)} %bitcast.6), calls=%async_computation.2 | async-start | bytes 8192 | tf_op jit(solution)/shard_map/all_to_all | solution.py:75
  228.8 7.7 %all-to-all-done.2 = f32[8,1,128]{2,1,0:T(1,128)S(1)} async-done(((f32[8,1,128]{2,1,0:T(1,128)}), f32[8,1,128]{2,1,0:T(1,128)S(1)}, u32[]{:S(2)}, u32[]{:S(2)}) %all-to-all-start.2) | async-done | bytes 4128 | tf_op jit(solution)/shard_map/all_to_all | solution.py:75
  236.5 3.4 %gather_fusion = f32[512]{0:T(512)} fusion(f32[1024]{0:T(1024)S(1)} %bitcast.31, s32[1024]{0:T(1024)S(1)} %pad_clamp_fusion), kind=kCustom, calls=%fused_computation | custom fusion | bytes 6144 | tf_op jit(solution)/shard_map/gather | solution.py:78
  (45 shorter events, 1.5 us)
Async XLA Ops:
  6.5 166.8 %all-gather.2.cloned.1.call-start = ((), (), s32[]{:S(2)}) async-start(), calls=%async_computation.3 | async-start | bytes 26738688 | tf_op jit(solution)/shard_map/all_gather | solution.py:68
  44.3 10.9 %all-to-all-start = ((bf16[8,1,128]{2,1,0:T(2,128)(2,1)}), bf16[8,1,128]{2,1,0:T(2,128)(2,1)S(1)}, u32[]{:S(2)}, u32[]{:S(2)}) async-start(bf16[8,1,128]{2,1,0:T(2,128)(2,1)} %compare_convert_fusion), calls=%async_computation | async-start | bytes 8192 | tf_op jit(solution)/shard_map/all_to_all | solution.py:62
  222.1 14.4 %all-to-all-start.2 = ((f32[8,1,128]{2,1,0:T(1,128)}), f32[8,1,128]{2,1,0:T(1,128)S(1)}, u32[]{:S(2)}, u32[]{:S(2)}) async-start(f32[8,1,128]{2,1,0:T(1,128)} %bitcast.6), calls=%async_computation.2 | async-start | bytes 8192 | tf_op jit(solution)/shard_map/all_to_all | solution.py:75
Sparse Core Ops, SparseCore 0:
  43.7 129.5 all-gather.1
where the time goes:
time: 247 us
  waiting for transfers between devices  113 us (46%)
  blocking collectives  50.1 us (20%)
  matrix products  49.6 us (20%)
  between operations  13.5 us (5%)
  starting transfers between devices  9.97 us (4%)
  other arithmetic  6.56 us (3%)
  local copies, waits for them, and re-layouts  3.74 us (2%)
    all_gather x1, waiting for transfers between devices, on_device(): column_rows = lax.all_gather(own_rows, 'row', axis=0, tiled=True)  97.8 us
    dot_general x8, matrix products, visit(): lax.dot_general(own_rows, piece_rows, (((1,), (1,)), ((), ())), preferred...  47.3 us
    all_to_all x1, blocking collectives, on_device(): lax.all_to_all(outgoing.reshape(groups, per_cluster, -1), 'group', split_...  29.7 us
    all_gather x1, blocking collectives, on_device(): column_flags = lax.all_gather(own_flags, 'row', axis=0, tiled=True)  20.3 us
    all_to_all x1, waiting for transfers between devices, on_device(): lax.all_to_all(nearest.reshape(groups, per_cluster), 'group', split_axis=...  7.65 us
    all_to_all x1, waiting for transfers between devices, on_device(): lax.all_to_all(filled, 'group', split_axis=0, concat_axis=0, tiled=True)  7.56 us
    all_to_all x1, starting transfers between devices, on_device(): lax.all_to_all(nearest.reshape(groups, per_cluster), 'group', split_axis=...  6.71 us
  transfers between devices with their start and end apart: 3, of which 3 were waited for; matrix products, arithmetic and copies ran while one was open for 0% of the time, Pallas kernels for 0%

commit v1 on v0

--- a/solution.py
+++ b/solution.py
@@ -65,7 +65,8 @@
     own_flags = arrived_flags.reshape(capacity)
     own_ids = lax.axis_index("row") * capacity + jnp.arange(capacity, dtype=jnp.int32)
     initial = jnp.full((capacity,), absent, jnp.float32)
-    column_rows = lax.all_gather(own_rows, "row", axis=0, tiled=True)
+    sent = jnp.stack([own_rows] * lax.axis_size("row"))
+    column_rows = jnp.concatenate(lax.all_to_all(sent, "row", 0, 0), axis=0)
     column_flags = lax.all_gather(own_flags, "row", axis=0, tiled=True)
     column_ids = jnp.arange(column_rows.shape[0], dtype=jnp.int32)
     found, unused_columns = block_maxima(

time: 247 us -> 405 us (1.64)
  blocking collectives: 50.1 us -> 312 us
  waiting for transfers between devices: 113 us -> 11 us
  between operations: 13.5 us -> 0.08 us
  local copies, waits for them, and re-layouts: 3.74 us -> 12.3 us
  starting transfers between devices: 9.97 us -> 15.9 us
    all_gather x1, blocking collectives: 20.3 us -> 286 us  [on_device(): column_flags = lax.all_gather(own_flags, 'row', axis=0, tiled=True)]
    all_gather x1 -> x0, waiting for transfers between devices: 97.8 us -> none  [on_device(): column_rows = lax.all_gather(own_rows, 'row', axis=0, tiled=True)]
    another operation x1 -> x2, local copies, waits for them, and re-layouts: 0.01 us -> 8.59 us  [the longest x1 8.58 us: on_device(): sent = jnp.stack([own_rows] * lax.axis_size('row'))]
    all_to_all x0 -> x1, starting transfers between devices: none -> 5.57 us  [on_device(): column_rows = jnp.concatenate(lax.all_to_all(sent, 'row', 0, 0), axis=0)]
    all_to_all x1, waiting for transfers between devices: 7.56 us -> 3.3 us  [on_device(): lax.all_to_all(filled, 'group', split_axis=0, concat_axis=0, tiled=True)]
  transfers between devices with their start and end apart: 3 -> 3, of which waited for: 3 -> 2; matrix products, arithmetic and copies ran while one was open for 0% -> 1% of each run, Pallas kernels for 0% -> 0%
where the time goes in v1:
time: 405 us; the launch traced here: 404 us
  blocking collectives  312 us (77%)
  matrix products  45.8 us (11%)
  starting transfers between devices  15.9 us (4%)
  local copies, waits for them, and re-layouts  12.3 us (3%)
  waiting for transfers between devices  11 us (3%)
  other arithmetic  6.57 us (2%)
    all_gather x1, blocking collectives, on_device(): column_flags = lax.all_gather(own_flags, 'row', axis=0, tiled=True)  286 us
    dot_general x8, matrix products, visit(): lax.dot_general(own_rows, piece_rows, (((1,), (1,)), ((), ())), preferred...  43.5 us
    all_to_all x1, blocking collectives, on_device(): lax.all_to_all(outgoing.reshape(groups, per_cluster, -1), 'group', split_...  26 us
    another operation x1, local copies, waits for them, and re-layouts, on_device(): sent = jnp.stack([own_rows] * lax.axis_size('row'))  8.58 us
  transfers between devices with their start and end apart: 3, of which 2 were waited for; matrix products, arithmetic and copies ran while one was open for 1% of the time, Pallas kernels for 0%

profile of v1, /device:TPU:0, one launch (start us, length us, event | category | flops | bytes accessed | tf_op | source)
XLA Modules:
  0.0 404.3 jit_solution(17635833564164960105)
XLA Ops:
  0.0 0.7 fusion.14
  0.7 1.1 reduce-window.6
  2.1 0.9 fusion.13
  3.6 7.0 %all-to-all-start = ((bf16[8,1,128]{2,1,0:T(2,128)(2,1)}), bf16[8,1,128]{2,1,0:T(2,128)(2,1)S(1)}, u32[]{:S(2)}, u32[]{:S(2)}) async-start(bf16[8,1,128]{2,1,0:T(2,128)(2,1)} %compare_convert_fusion), calls=%async_computation | async-start | bytes 8192 | tf_op jit(solution)/shard_map/all_to_all | solution.py:62
  10.6 0.7 compare_select_fusion
  11.3 1.4 fusion.8
  12.7 2.3 fusion.7
  15.0 3.3 all-to-all-done
  18.3 26.0 %all_to_all.25 = bf16[8,128,768]{2,1,0:T(8,128)(2,1)S(1)} all-to-all(bf16[8,128,768]{2,1,0:T(8,128)(2,1)S(1)} %bitcast.34), channel_id=1, replica_groups=mesh['group'=8,'row'=16] {'group'}, dimensions={0} | all-to-all | bytes 3145728 | tf_op jit(solution)/shard_map/all_to_all | solution.py:55
  44.3 8.6 %stack.3 = bf16[16,1024,768]{2,1,0:T(8,128)(2,1)} broadcast(bf16[1024,768]{1,0:T(8,128)(2,1)S(1)} %bitcast.32), dimensions={1,2} | broadcast | bytes 26738688 | tf_op jit(solution)/shard_map/stack | solution.py:68
  52.9 5.6 %all-to-all-start.2 = ((bf16[16,1024,768]{2,1,0:T(8,128)(2,1)}), bf16[16,1024,768]{2,1,0:T(8,128)(2,1)}, u32[]{:S(2)}, u32[]{:S(2)}) async-start(bf16[16,1024,768]{2,1,0:T(8,128)(2,1)} %stack.3), calls=%async_computation.2 | async-start | bytes 50331648 | tf_op jit(solution)/shard_map/all_to_all | solution.py:69
  58.5 286.3 %all_gather.3 = bf16[16384]{0:T(1024)(128)(2,1)S(1)} all-gather(bf16[1024]{0:T(1024)(128)(2,1)S(1)} %bitcast.37), channel_id=1, replica_groups=mesh['group'=8,'row'=16] {'row'}, dimensions={0}, use_global_device_ids=true | all-gather | bytes 34816 | tf_op jit(solution)/shard_map/all_gather | solution.py:70
  344.9 44.4 %while.11 = (s32[]{:T(128)}, f32[1024]{0:T(1024)S(1)}, pred[1024]{0:T(1024)(128)(4,1)S(1)}, bf16[8,2048]{1,0:T(8,128)(2,1)S(1)}, s32[8,2048]{1,0:T(8,128)S(1)}, ...) while((s32[]{:T(128)}, f32[1024]{0:T(1024)S(1)}, ...), condition=%wide.region_7.8_spmd.clone, body=%wide.region_5.7_spmd.clone.sunk | while | flops 3231719424 | bytes 4777595 | solution.py:30
  344.9 5.4 %fusion.21 = f32[1024]{0:T(1024)S(1)} fusion(bf16[1024,768]{1,0:T(8,128)(2,1)S(1)} %get-tuple-element.173, s32[1024]{0:T(1024)S(1)} %iota_add_fusion.2, s32[2048]{0:T(1024)S(1)} %bitcast.35, pred[1024]{0:T(1024)(128)(4,1)S(1)} %get-tuple-element.169, pred[2048]{0:T(1024)(128)(4,1)S(1)} %compare_reduce_fusion.2, ...), kind=kOutput, calls=%fused_computation.3.clone.1 | convolution fusion | flops 3231710208 | bytes 4738560 | tf_op jit(solution)/shard_map/while/body/eval_jaxpr/dot_general | solution.py:20
  350.5 5.4 %fusion.21 = f32[1024]{0:T(1024)S(1)} fusion(bf16[1024,768]{1,0:T(8,128)(2,1)S(1)} %get-tuple-element.173, s32[1024]{0:T(1024)S(1)} %iota_add_fusion.2, s32[2048]{0:T(1024)S(1)} %bitcast.35, pred[1024]{0:T(1024)(128)(4,1)S(1)} %get-tuple-element.169, pred[2048]{0:T(1024)(128)(4,1)S(1)} %compare_reduce_fusion.2, ...), kind=kOutput, calls=%fused_computation.3.clone.1 | convolution fusion | flops 3231710208 | bytes 4738560 | tf_op jit(solution)/shard_map/while/body/eval_jaxpr/dot_general | solution.py:20
  356.1 5.4 %fusion.21 = f32[1024]{0:T(1024)S(1)} fusion(bf16[1024,768]{1,0:T(8,128)(2,1)S(1)} %get-tuple-element.173, s32[1024]{0:T(1024)S(1)} %iota_add_fusion.2, s32[2048]{0:T(1024)S(1)} %bitcast.35, pred[1024]{0:T(1024)(128)(4,1)S(1)} %get-tuple-element.169, pred[2048]{0:T(1024)(128)(4,1)S(1)} %compare_reduce_fusion.2, ...), kind=kOutput, calls=%fused_computation.3.clone.1 | convolution fusion | flops 3231710208 | bytes 4738560 | tf_op jit(solution)/shard_map/while/body/eval_jaxpr/dot_general | solution.py:20
  361.6 5.4 %fusion.21 = f32[1024]{0:T(1024)S(1)} fusion(bf16[1024,768]{1,0:T(8,128)(2,1)S(1)} %get-tuple-element.173, s32[1024]{0:T(1024)S(1)} %iota_add_fusion.2, s32[2048]{0:T(1024)S(1)} %bitcast.35, pred[1024]{0:T(1024)(128)(4,1)S(1)} %get-tuple-element.169, pred[2048]{0:T(1024)(128)(4,1)S(1)} %compare_reduce_fusion.2, ...), kind=kOutput, calls=%fused_computation.3.clone.1 | convolution fusion | flops 3231710208 | bytes 4738560 | tf_op jit(solution)/shard_map/while/body/eval_jaxpr/dot_general | solution.py:20
  367.2 5.4 %fusion.21 = f32[1024]{0:T(1024)S(1)} fusion(bf16[1024,768]{1,0:T(8,128)(2,1)S(1)} %get-tuple-element.173, s32[1024]{0:T(1024)S(1)} %iota_add_fusion.2, s32[2048]{0:T(1024)S(1)} %bitcast.35, pred[1024]{0:T(1024)(128)(4,1)S(1)} %get-tuple-element.169, pred[2048]{0:T(1024)(128)(4,1)S(1)} %compare_reduce_fusion.2, ...), kind=kOutput, calls=%fused_computation.3.clone.1 | convolution fusion | flops 3231710208 | bytes 4738560 | tf_op jit(solution)/shard_map/while/body/eval_jaxpr/dot_general | solution.py:20
  372.7 5.4 %fusion.21 = f32[1024]{0:T(1024)S(1)} fusion(bf16[1024,768]{1,0:T(8,128)(2,1)S(1)} %get-tuple-element.173, s32[1024]{0:T(1024)S(1)} %iota_add_fusion.2, s32[2048]{0:T(1024)S(1)} %bitcast.35, pred[1024]{0:T(1024)(128)(4,1)S(1)} %get-tuple-element.169, pred[2048]{0:T(1024)(128)(4,1)S(1)} %compare_reduce_fusion.2, ...), kind=kOutput, calls=%fused_computation.3.clone.1 | convolution fusion | flops 3231710208 | bytes 4738560 | tf_op jit(solution)/shard_map/while/body/eval_jaxpr/dot_general | solution.py:20
  378.3 5.4 %fusion.21 = f32[1024]{0:T(1024)S(1)} fusion(bf16[1024,768]{1,0:T(8,128)(2,1)S(1)} %get-tuple-element.173, s32[1024]{0:T(1024)S(1)} %iota_add_fusion.2, s32[2048]{0:T(1024)S(1)} %bitcast.35, pred[1024]{0:T(1024)(128)(4,1)S(1)} %get-tuple-element.169, pred[2048]{0:T(1024)(128)(4,1)S(1)} %compare_reduce_fusion.2, ...), kind=kOutput, calls=%fused_computation.3.clone.1 | convolution fusion | flops 3231710208 | bytes 4738560 | tf_op jit(solution)/shard_map/while/body/eval_jaxpr/dot_general | solution.py:20
  383.8 5.4 %fusion.21 = f32[1024]{0:T(1024)S(1)} fusion(bf16[1024,768]{1,0:T(8,128)(2,1)S(1)} %get-tuple-element.173, s32[1024]{0:T(1024)S(1)} %iota_add_fusion.2, s32[2048]{0:T(1024)S(1)} %bitcast.35, pred[1024]{0:T(1024)(128)(4,1)S(1)} %get-tuple-element.169, pred[2048]{0:T(1024)(128)(4,1)S(1)} %compare_reduce_fusion.2, ...), kind=kOutput, calls=%fused_computation.3.clone.1 | convolution fusion | flops 3231710208 | bytes 4738560 | tf_op jit(solution)/shard_map/while/body/eval_jaxpr/dot_general | solution.py:20
  389.9 3.3 all-to-all-start.3
  393.3 7.6 %all-to-all-done.3 = f32[8,1,128]{2,1,0:T(1,128)S(1)} async-done(((f32[8,1,128]{2,1,0:T(1,128)}), f32[8,1,128]{2,1,0:T(1,128)S(1)}, u32[]{:S(2)}, u32[]{:S(2)}) %all-to-all-start.3) | async-done | bytes 4128 | tf_op jit(solution)/shard_map/all_to_all | solution.py:76
  400.9 3.4 gather_fusion
  (45 shorter events, 2.2 us)
Async XLA Ops:
  3.6 14.7 %all-to-all-start = ((bf16[8,1,128]{2,1,0:T(2,128)(2,1)}), bf16[8,1,128]{2,1,0:T(2,128)(2,1)S(1)}, u32[]{:S(2)}, u32[]{:S(2)}) async-start(bf16[8,1,128]{2,1,0:T(2,128)(2,1)} %compare_convert_fusion), calls=%async_computation | async-start | bytes 8192 | tf_op jit(solution)/shard_map/all_to_all | solution.py:62
  52.9 292.0 %all-to-all-start.2 = ((bf16[16,1024,768]{2,1,0:T(8,128)(2,1)}), bf16[16,1024,768]{2,1,0:T(8,128)(2,1)}, u32[]{:S(2)}, u32[]{:S(2)}) async-start(bf16[16,1024,768]{2,1,0:T(8,128)(2,1)} %stack.3), calls=%async_computation.2 | async-start | bytes 50331648 | tf_op jit(solution)/shard_map/all_to_all | solution.py:69
  389.9 11.0 %all-to-all-start.3 = ((f32[8,1,128]{2,1,0:T(1,128)}), f32[8,1,128]{2,1,0:T(1,128)S(1)}, u32[]{:S(2)}, u32[]{:S(2)}) async-start(f32[8,1,128]{2,1,0:T(1,128)} %bitcast.6), calls=%async_computation.3 | async-start | bytes 8192 | tf_op jit(solution)/shard_map/all_to_all | solution.py:76
